TPU v7x, 32 devices: a whole 2x2x4 slice. The times are simulated.
32 devices in a mesh: grp: 2 (over y), br: 8 (over z, x), sub: 2 (over core).
Axes of the slice: x: 2, y: 2, z: 4, core: 2. Of those that a mesh axis runs over, the one named last changes fastest.
Arguments:
- charges: bfloat16 [32, 131072], P(None, ('grp', 'br', 'sub')), parts along dimension 1, may hold values from -6 to 6
- order: int32 [131072], P(('grp', 'br', 'sub')), parts along dimension 0, may hold values from 0 to 8191, as said below
- coords: float32 [3, 131072], P(None, ('grp', 'br', 'sub')), parts along dimension 1, may hold values from 0 to 1
- leaf_basis: bfloat16 [1024, 64, 128], P(('grp', 'br', 'sub')), parts along dimension 0, may hold values from -0.5 to 0.5
- leaf_transfer: bfloat16 [1024, 64, 64], P(('grp', 'br', 'sub')), parts along dimension 0, may hold values from -0.375 to 0.375
- branch_transfer: bfloat16 [16, 64, 64], P(('grp', 'br')), parts along dimension 0, may hold values from -0.75 to 0.75
- upper_transfer: bfloat16 [8, 64, 64], P('grp'), parts along dimension 0, may hold values from -0.75 to 0.75
- top_skeleton: float32 [3, 1792], P(None, 'grp'), parts along dimension 1, may hold values from 0 to 1
- near_src: int32 [1024, 27], P(('grp', 'br', 'sub')), parts along dimension 0, may hold values from 0 to 511, as said below
- near_count: int32 [1024], P(('grp', 'br', 'sub')), parts along dimension 0, may hold values from 14 to 27
- far_src: int32 [1024, 6], P(('grp', 'br', 'sub')), parts along dimension 0, may hold values from 0 to 511, as said below
- far_count: int32 [1024], P(('grp', 'br', 'sub')), parts along dimension 0, may hold values from 1 to 6
- top_src: int32 [28, 6], P('grp'), parts along dimension 0, may hold values from 0 to 7, as said below
- top_count: int32 [28], P('grp'), parts along dimension 0, may hold values from 1 to 6
Outputs:
- potential: float32 [32, 131072], P(None, ('grp', 'br', 'sub')), parts along dimension 1
There are 2 independent parts, one for each index of `grp`. A program takes and returns all parts, laid end to end along the dimension named above; each array names one. Nothing has to cross between parts.
Inputs may be any that keep to these rules, and one draw needn't show every extreme that they name: `order`: within each branch the 8192 entries form a permutation: every input position of the branch (its first device's columns first) appears once. `near_src`: entry 0 of each list is the leaf itself; every source lies within 32 leaves of its target; entries at positions near_count or beyond are to be ignored. `far_src`: every source lies within 32 leaves of its target and differs from it; entries at positions far_count or beyond are to be ignored. `top_src`: rows 0 to 7 belong to the branches, the next 4 rows to the level above, the last 2 rows to the level above that; entries are node numbers within the row's level and never the row's own node; entries at positions top_count or beyond are to be ignored.
All inputs are finite; a program needn't handle non-finite values.
Results may differ from a plain program's by a relative error of at most 0.0047.
Values may be sent and summed in bfloat16 or wider, within the bound.
No kernel may reach another device: no remote copies, remote signals or barrier semaphores. Data moves between devices by JAX's collectives and lax.ppermute only.
A program may use at most 64 MiB of HBM per device.

v0:
```python
import math

import jax
import jax.numpy as jnp
from jax import lax
from jax.sharding import PartitionSpec as P

length_scale = 0.25
root_three = 1.7320508075688772


def extended(cells, sides, width):
    for axis, dim in sides:
        count = lax.axis_size(axis)
        ends = count - 1
        head = lax.slice_in_dim(cells, 0, width, axis=dim)
        tail = lax.slice_in_dim(cells, cells.shape[dim] - width, cells.shape[dim], axis=dim)
        cells = jnp.concatenate(
            [
                lax.ppermute(tail, axis, [(i, (i + 1) % count) for i in range(ends)]),
                cells,
                lax.ppermute(head, axis, [((i + 1) % count, i) for i in range(ends)]),
            ],
            axis=dim,
        )
    return cells


def matern(sources, targets):
    gap_first = sources[..., 0, :, None] - targets[..., 0, None, :]
    gap_second = sources[..., 1, :, None] - targets[..., 1, None, :]
    gap_third = sources[..., 2, :, None] - targets[..., 2, None, :]
    squared = gap_first * gap_first + gap_second * gap_second + gap_third * gap_third
    scaled = root_three / length_scale * jnp.sqrt(squared)
    return (1.0 + scaled) * jnp.exp(-scaled)


def node_field(source_places, target_places, source_coef, live_count):
    kernel = matern(source_places, target_places[None])
    validity = (jnp.arange(source_places.shape[0], dtype=jnp.int32) < live_count).astype(
        jnp.float32
    )
    return jnp.einsum(
        "fqp,fqn->pn",
        kernel * validity[:, None, None],
        source_coef,
        precision=lax.Precision.HIGHEST,
    )


def shards(
    charges,
    order,
    coords,
    leaf_basis,
    leaf_transfer,
    branch_transfer,
    upper_transfer,
    top_skeleton,
    near_src,
    near_count,
    far_src,
    far_count,
    top_src,
    top_count,
):
    highest = lax.Precision.HIGHEST
    rhs_width = charges.shape[0]
    leaf_local, basis_rank, leaf_points = leaf_basis.shape
    branches = lax.axis_size("br")
    branch = lax.axis_index("br")
    branch_charges = lax.all_gather(charges, "sub", axis=1, tiled=True)
    tree_charges = jnp.take(branch_charges, order, axis=1).reshape(
        rhs_width, leaf_local, leaf_points
    )
    tree_rows = tree_charges.transpose(1, 0, 2)
    places = coords.reshape(3, leaf_local, leaf_points).transpose(1, 0, 2)
    leaf_coef = jnp.einsum(
        "lrp,lnp->lrn", leaf_basis, tree_rows, preferred_element_type=jnp.float32
    ).astype(jnp.bfloat16)
    packed = jnp.concatenate(
        [
            places.reshape(leaf_local, 3 * leaf_points),
            leaf_coef.astype(jnp.float32).reshape(leaf_local, basis_rank * rhs_width),
        ],
        axis=1,
    )
    wide_rows = extended(
        tree_rows.reshape(leaf_local, rhs_width * leaf_points), ((("br", "sub"), 0),), leaf_local
    )
    wide_charges = wide_rows.reshape(3 * leaf_local, rhs_width, leaf_points)
    wide_pack = extended(packed, ((("br", "sub"), 0),), leaf_local)
    wide_places = wide_pack[:, : 3 * leaf_points].reshape(3 * leaf_local, 3, leaf_points)
    wide_coef = (
        wide_pack[:, 3 * leaf_points :]
        .reshape(3 * leaf_local, basis_rank, rhs_width)
        .astype(jnp.bfloat16)
    )
    first_leaf = (lax.axis_index(("br", "sub")) - 1) * leaf_local
    device_up = jnp.einsum(
        "lrs,lrn->sn", leaf_transfer, leaf_coef, preferred_element_type=jnp.float32
    )
    own_transfer = branch_transfer[0].astype(jnp.float32)
    lifted = jnp.dot(own_transfer.T, device_up, precision=highest)
    every_up, every_lift = (
        lax.all_gather(device_up.reshape(1, -1), ("br", "sub"), axis=0, tiled=True),
        lax.all_gather(lifted.reshape(1, -1), ("br", "sub"), axis=0, tiled=True),
    )
    branch_coef = every_up.reshape(branches, -1, basis_rank, rhs_width).sum(axis=1)
    lift_terms = every_lift.reshape(branches, -1, basis_rank, rhs_width).sum(axis=1)
    level_one = lift_terms.reshape(branches // 2, 2, basis_rank, rhs_width).sum(axis=1)
    level_two = jnp.einsum(
        "prs,prn->psn", upper_transfer.astype(jnp.float32), level_one, precision=highest
    )
    level_two = level_two.reshape(branches // 4, 2, basis_rank, rhs_width).sum(axis=1)
    top_nodes = top_src.shape[0]
    skeleton = top_skeleton.reshape(3, top_nodes, basis_rank).transpose(1, 0, 2)

    def own_field(coef, offset, node):
        sources = top_src[offset + node]
        return node_field(
            skeleton[offset + sources],
            skeleton[offset + node],
            coef[sources],
            top_count[offset + node],
        )

    parent = branch // 2
    grandparent = branch // 4
    field_zero = own_field(branch_coef, 0, branch)
    field_one = own_field(level_one, branches, parent)
    field_two = own_field(level_two, branches + branches // 2, grandparent)
    down_one = field_one + jnp.dot(
        upper_transfer[parent].astype(jnp.float32), field_two, precision=highest
    )
    down_zero = (field_zero + jnp.dot(own_transfer, down_one, precision=highest)).astype(
        jnp.bfloat16
    )
    far_local = far_src - first_leaf
    far_valid = (
        jnp.arange(far_src.shape[1], dtype=jnp.int32)[None, :] < far_count[:, None]
    ).astype(jnp.bfloat16)
    far_kernel = (
        matern(wide_places[far_local][..., :basis_rank], places[:, None, :, :basis_rank]).astype(
            jnp.bfloat16
        )
        * far_valid[:, :, None, None]
    )
    leaf_field = jnp.einsum(
        "lfqp,lfqn->lpn", far_kernel, wide_coef[far_local], preferred_element_type=jnp.float32
    )
    leaf_down = (
        leaf_field
        + jnp.einsum("lrs,sn->lrn", leaf_transfer, down_zero, preferred_element_type=jnp.float32)
    ).astype(jnp.bfloat16)
    far_part = jnp.einsum("lrn,lrp->lnp", leaf_down, leaf_basis, preferred_element_type=jnp.float32)
    near_local = near_src - first_leaf
    near_valid = (
        jnp.arange(near_src.shape[1], dtype=jnp.int32)[None, :] < near_count[:, None]
    ).astype(jnp.bfloat16)
    block_size = math.gcd(leaf_local, 2)
    block_count = leaf_local // block_size

    def near_block(inputs):
        targets, sources, validity = inputs
        kernel = (
            matern(wide_places[sources], targets[:, None]).astype(jnp.bfloat16)
            * validity[:, :, None, None]
        )
        gathered = wide_charges[sources]
        return jnp.einsum("ljnq,ljqp->lnp", gathered, kernel, preferred_element_type=jnp.float32)

    near_parts = lax.map(
        near_block,
        (
            places.reshape(block_count, block_size, 3, leaf_points),
            near_local.reshape(block_count, block_size, -1),
            near_valid.reshape(block_count, block_size, -1),
        ),
    )
    near_part = near_parts.reshape(leaf_local, rhs_width, leaf_points)
    return (near_part + far_part).transpose(1, 0, 2).reshape(rhs_width, leaf_local * leaf_points)


def solution(mesh):
    return jax.shard_map(
        shards,
        mesh=mesh,
        in_specs=(
            P(None, ("grp", "br", "sub")),
            P(("grp", "br", "sub")),
            P(None, ("grp", "br", "sub")),
            P(("grp", "br", "sub"), None, None),
            P(("grp", "br", "sub"), None, None),
            P(("grp", "br"), None, None),
            P("grp", None, None),
            P(None, "grp"),
            P(("grp", "br", "sub"), None),
            P(("grp", "br", "sub")),
            P(("grp", "br", "sub"), None),
            P(("grp", "br", "sub")),
            P("grp", None),
            P("grp"),
        ),
        out_specs=P(None, ("grp", "br", "sub")),
        check_vma=False,
    )
```

profile of v0, /device:TPU:1, one launch (start us, length us, event | category | flops | bytes accessed | tf_op | source)
XLA Modules:
  0.0 279.2 jit_solution(13392462973341071746)
XLA Ops:
  0.0 0.8 fusion.105
  1.5 2.3 copy.144
  3.8 3.5 %all_gather.9 = bf16[32,8192]{0,1:T(8,128)(2,1)S(1)} all-gather(bf16[32,4096]{0,1:T(8,128)(2,1)} %copy.144), channel_id=1, replica_groups=mesh['grp'=2,'br'=8,'sub'=2] {'sub'}, dimensions={1}, use_global_device_ids=true | all-gather | bytes 786432 | tf_op jit(solution)/shard_map/all_gather | solution.py:72
  7.3 15.0 %gather_fusion.2 = bf16[4096,32]{1,0:T(8,128)(2,1)} fusion(bf16[32,8192]{0,1:T(8,128)(2,1)S(1)} %all_gather.9, s32[4096]{0:T(1024)S(1)} %fusion.105), kind=kCustom, calls=%fused_computation.2 | custom fusion | bytes 540672 | tf_op jit(solution)/shard_map/jit(_take)/gather | solution.py:73
  22.3 1.6 copy.145
  25.1 4.5 %collective-permute-start.2 = (f32[32,2432]{1,0:T(8,128)S(1)}, f32[32,2432]{1,0:T(8,128)S(1)}, u32[]{:S(2)}, u32[]{:S(2)}) collective-permute-start(f32[32,2432]{1,0:T(8,128)S(1)} %constant_dynamic-update-slice_fusion), channel_id=1, source_target_pairs={{0,1},{1,2},{2,3},{3,4},{4,5},{5,6},{6,7},{7,8},{8,9},{9,10},{10,1... | collective-permute-start | bytes 933896 | tf_op jit(solution)/shard_map/ppermute | solution.py:20
  29.6 1.9 collective-permute-start.3
  31.7 3.6 %collective-permute-start = (bf16[32,4096]{1,0:T(8,128)(2,1)S(1)}, bf16[32,4096]{1,0:T(8,128)(2,1)}, u32[]{:S(2)}, u32[]{:S(2)}) collective-permute-start(bf16[32,4096]{1,0:T(8,128)(2,1)S(1)} %bitcast.284), channel_id=1, source_target_pairs={{0,1},{1,2},{2,3},{3,4},{4,5},{5,6},{6,7},{7,8},{8,9},{9,10},{10,1... | collective-permute-start | bytes 786440 | tf_op jit(solution)/shard_map/ppermute | solution.py:20
  35.3 1.9 collective-permute-start.1
  37.3 0.8 fusion.149
  38.1 0.8 reshape.331
  39.5 1.0 dynamic-slice_reduce_fusion
  41.7 22.4 %all-gather.1 = f32[16,1,2048]{2,1,0:T(1,128)S(1)} all-gather(f32[1,1,2048]{2,1,0:T(1,128)S(1)} %reshape.438), channel_id=1, replica_groups=mesh['grp'=2,'br'=8,'sub'=2] {'br','sub'}, dimensions={0}, use_global_device_ids=true | all-gather | bytes 139264 | tf_op jit(solution)/shard_map/all_gather | solution.py:107
  67.8 1.2 compare_convert_fusion.2
  72.3 1.1 compare_convert_fusion.1
  74.1 18.0 %all-gather = f32[16,1,2048]{2,1,0:T(1,128)S(1)} all-gather(f32[1,1,2048]{2,1,0:T(1,128)S(1)} %reshape.436), channel_id=1, replica_groups=mesh['grp'=2,'br'=8,'sub'=2] {'br','sub'}, dimensions={0}, use_global_device_ids=true | all-gather | bytes 139264 | tf_op jit(solution)/shard_map/all_gather | solution.py:106
  95.6 1.3 broadcast_subtract_fusion
  96.9 0.7 lt.165
  101.0 1.2 convolution_bitcast_fusion.3
  102.2 1.2 convolution_bitcast_fusion.2
  104.1 0.8 fusion.26
  106.1 1.0 copy.189
  107.5 0.9 gather_fusion.3
  108.4 0.9 fusion.126
  110.2 1.4 copy.157
  111.6 2.0 gather_fusion.4
  113.6 151.0 %while.10 = (s32[]{:T(128)}, f32[16,2,32,128]{3,2,1,0:T(8,128)}, s32[16,2,27]{2,1,0:T(2,128)}, bf16[96,32,128]{2,1,0:T(8,128)(2,1)S(1)}, f32[96,3,128]{2,1,0:T(4...) while((s32[]{:T(128)}, f32[16,2,32,128]{3,2,1,0:T(8,128)}, ...), condition=%wide.region_1.2_spmd, body=%wide.region_0.1_spmd.sunk | while | flops 69010592 | bytes 2154921 | solution.py:173
  113.6 0.8 compare_select_fusion.10
  116.5 0.8 gather_fusion
  118.6 4.6 %fusion.160 = f32[16,2,32,128]{3,2,1,0:T(8,128)} fusion(f32[16,2,32,128]{3,2,1,0:T(8,128)} %get-tuple-element.223, s32[]{:T(128)} %get-tuple-element.222, bf16[2,27,32,128]{3,2,1,0:T(8,128)(2,1)S(1)} %bitcast.270, f32[2,128]{1,0:T(2,128)S(1)} %get-tuple-element.206, f32[2,27,128]{2,1,0:T(8,128)S(1)} %copy.239, f32[2,128]{1,0:T(2,128)S(1)} %get-tuple-element.210, ...), kind=kOutput, calls=%fused_computation.15.clone.1 | convolution fusion | flops 69009408 | bytes 572012 | tf_op jit(solution)/shard_map/while/body/eval_jaxpr/ljnq,ljqp->lnp/dot_general | solution.py:171
  126.0 0.8 gather_fusion
  128.0 4.6 %fusion.160 = f32[16,2,32,128]{3,2,1,0:T(8,128)} fusion(f32[16,2,32,128]{3,2,1,0:T(8,128)} %get-tuple-element.223, s32[]{:T(128)} %get-tuple-element.222, bf16[2,27,32,128]{3,2,1,0:T(8,128)(2,1)S(1)} %bitcast.270, f32[2,128]{1,0:T(2,128)S(1)} %get-tuple-element.206, f32[2,27,128]{2,1,0:T(8,128)S(1)} %copy.239, f32[2,128]{1,0:T(2,128)S(1)} %get-tuple-element.210, ...), kind=kOutput, calls=%fused_computation.15.clone.1 | convolution fusion | flops 69009408 | bytes 572012 | tf_op jit(solution)/shard_map/while/body/eval_jaxpr/ljnq,ljqp->lnp/dot_general | solution.py:171
  135.3 0.8 gather_fusion
  137.4 4.6 %fusion.160 = f32[16,2,32,128]{3,2,1,0:T(8,128)} fusion(f32[16,2,32,128]{3,2,1,0:T(8,128)} %get-tuple-element.223, s32[]{:T(128)} %get-tuple-element.222, bf16[2,27,32,128]{3,2,1,0:T(8,128)(2,1)S(1)} %bitcast.270, f32[2,128]{1,0:T(2,128)S(1)} %get-tuple-element.206, f32[2,27,128]{2,1,0:T(8,128)S(1)} %copy.239, f32[2,128]{1,0:T(2,128)S(1)} %get-tuple-element.210, ...), kind=kOutput, calls=%fused_computation.15.clone.1 | convolution fusion | flops 69009408 | bytes 572012 | tf_op jit(solution)/shard_map/while/body/eval_jaxpr/ljnq,ljqp->lnp/dot_general | solution.py:171
  144.7 0.8 gather_fusion
  146.9 4.6 %fusion.160 = f32[16,2,32,128]{3,2,1,0:T(8,128)} fusion(f32[16,2,32,128]{3,2,1,0:T(8,128)} %get-tuple-element.223, s32[]{:T(128)} %get-tuple-element.222, bf16[2,27,32,128]{3,2,1,0:T(8,128)(2,1)S(1)} %bitcast.270, f32[2,128]{1,0:T(2,128)S(1)} %get-tuple-element.206, f32[2,27,128]{2,1,0:T(8,128)S(1)} %copy.239, f32[2,128]{1,0:T(2,128)S(1)} %get-tuple-element.210, ...), kind=kOutput, calls=%fused_computation.15.clone.1 | convolution fusion | flops 69009408 | bytes 572012 | tf_op jit(solution)/shard_map/while/body/eval_jaxpr/ljnq,ljqp->lnp/dot_general | solution.py:171
  154.2 0.8 gather_fusion
  156.2 4.6 %fusion.160 = f32[16,2,32,128]{3,2,1,0:T(8,128)} fusion(f32[16,2,32,128]{3,2,1,0:T(8,128)} %get-tuple-element.223, s32[]{:T(128)} %get-tuple-element.222, bf16[2,27,32,128]{3,2,1,0:T(8,128)(2,1)S(1)} %bitcast.270, f32[2,128]{1,0:T(2,128)S(1)} %get-tuple-element.206, f32[2,27,128]{2,1,0:T(8,128)S(1)} %copy.239, f32[2,128]{1,0:T(2,128)S(1)} %get-tuple-element.210, ...), kind=kOutput, calls=%fused_computation.15.clone.1 | convolution fusion | flops 69009408 | bytes 572012 | tf_op jit(solution)/shard_map/while/body/eval_jaxpr/ljnq,ljqp->lnp/dot_general | solution.py:171
  163.6 0.8 gather_fusion
  165.7 4.6 %fusion.160 = f32[16,2,32,128]{3,2,1,0:T(8,128)} fusion(f32[16,2,32,128]{3,2,1,0:T(8,128)} %get-tuple-element.223, s32[]{:T(128)} %get-tuple-element.222, bf16[2,27,32,128]{3,2,1,0:T(8,128)(2,1)S(1)} %bitcast.270, f32[2,128]{1,0:T(2,128)S(1)} %get-tuple-element.206, f32[2,27,128]{2,1,0:T(8,128)S(1)} %copy.239, f32[2,128]{1,0:T(2,128)S(1)} %get-tuple-element.210, ...), kind=kOutput, calls=%fused_computation.15.clone.1 | convolution fusion | flops 69009408 | bytes 572012 | tf_op jit(solution)/shard_map/while/body/eval_jaxpr/ljnq,ljqp->lnp/dot_general | solution.py:171
  173.0 0.8 gather_fusion
  175.2 4.6 %fusion.160 = f32[16,2,32,128]{3,2,1,0:T(8,128)} fusion(f32[16,2,32,128]{3,2,1,0:T(8,128)} %get-tuple-element.223, s32[]{:T(128)} %get-tuple-element.222, bf16[2,27,32,128]{3,2,1,0:T(8,128)(2,1)S(1)} %bitcast.270, f32[2,128]{1,0:T(2,128)S(1)} %get-tuple-element.206, f32[2,27,128]{2,1,0:T(8,128)S(1)} %copy.239, f32[2,128]{1,0:T(2,128)S(1)} %get-tuple-element.210, ...), kind=kOutput, calls=%fused_computation.15.clone.1 | convolution fusion | flops 69009408 | bytes 572012 | tf_op jit(solution)/shard_map/while/body/eval_jaxpr/ljnq,ljqp->lnp/dot_general | solution.py:171
  182.5 0.8 gather_fusion
  184.5 4.6 %fusion.160 = f32[16,2,32,128]{3,2,1,0:T(8,128)} fusion(f32[16,2,32,128]{3,2,1,0:T(8,128)} %get-tuple-element.223, s32[]{:T(128)} %get-tuple-element.222, bf16[2,27,32,128]{3,2,1,0:T(8,128)(2,1)S(1)} %bitcast.270, f32[2,128]{1,0:T(2,128)S(1)} %get-tuple-element.206, f32[2,27,128]{2,1,0:T(8,128)S(1)} %copy.239, f32[2,128]{1,0:T(2,128)S(1)} %get-tuple-element.210, ...), kind=kOutput, calls=%fused_computation.15.clone.1 | convolution fusion | flops 69009408 | bytes 572012 | tf_op jit(solution)/shard_map/while/body/eval_jaxpr/ljnq,ljqp->lnp/dot_general | solution.py:171
  191.8 0.8 gather_fusion
  193.9 4.6 %fusion.160 = f32[16,2,32,128]{3,2,1,0:T(8,128)} fusion(f32[16,2,32,128]{3,2,1,0:T(8,128)} %get-tuple-element.223, s32[]{:T(128)} %get-tuple-element.222, bf16[2,27,32,128]{3,2,1,0:T(8,128)(2,1)S(1)} %bitcast.270, f32[2,128]{1,0:T(2,128)S(1)} %get-tuple-element.206, f32[2,27,128]{2,1,0:T(8,128)S(1)} %copy.239, f32[2,128]{1,0:T(2,128)S(1)} %get-tuple-element.210, ...), kind=kOutput, calls=%fused_computation.15.clone.1 | convolution fusion | flops 69009408 | bytes 572012 | tf_op jit(solution)/shard_map/while/body/eval_jaxpr/ljnq,ljqp->lnp/dot_general | solution.py:171
  201.2 0.8 gather_fusion
  203.3 4.6 %fusion.160 = f32[16,2,32,128]{3,2,1,0:T(8,128)} fusion(f32[16,2,32,128]{3,2,1,0:T(8,128)} %get-tuple-element.223, s32[]{:T(128)} %get-tuple-element.222, bf16[2,27,32,128]{3,2,1,0:T(8,128)(2,1)S(1)} %bitcast.270, f32[2,128]{1,0:T(2,128)S(1)} %get-tuple-element.206, f32[2,27,128]{2,1,0:T(8,128)S(1)} %copy.239, f32[2,128]{1,0:T(2,128)S(1)} %get-tuple-element.210, ...), kind=kOutput, calls=%fused_computation.15.clone.1 | convolution fusion | flops 69009408 | bytes 572012 | tf_op jit(solution)/shard_map/while/body/eval_jaxpr/ljnq,ljqp->lnp/dot_general | solution.py:171
  210.7 0.8 gather_fusion
  212.8 4.6 %fusion.160 = f32[16,2,32,128]{3,2,1,0:T(8,128)} fusion(f32[16,2,32,128]{3,2,1,0:T(8,128)} %get-tuple-element.223, s32[]{:T(128)} %get-tuple-element.222, bf16[2,27,32,128]{3,2,1,0:T(8,128)(2,1)S(1)} %bitcast.270, f32[2,128]{1,0:T(2,128)S(1)} %get-tuple-element.206, f32[2,27,128]{2,1,0:T(8,128)S(1)} %copy.239, f32[2,128]{1,0:T(2,128)S(1)} %get-tuple-element.210, ...), kind=kOutput, calls=%fused_computation.15.clone.1 | convolution fusion | flops 69009408 | bytes 572012 | tf_op jit(solution)/shard_map/while/body/eval_jaxpr/ljnq,ljqp->lnp/dot_general | solution.py:171
  220.2 0.8 gather_fusion
  222.3 4.6 %fusion.160 = f32[16,2,32,128]{3,2,1,0:T(8,128)} fusion(f32[16,2,32,128]{3,2,1,0:T(8,128)} %get-tuple-element.223, s32[]{:T(128)} %get-tuple-element.222, bf16[2,27,32,128]{3,2,1,0:T(8,128)(2,1)S(1)} %bitcast.270, f32[2,128]{1,0:T(2,128)S(1)} %get-tuple-element.206, f32[2,27,128]{2,1,0:T(8,128)S(1)} %copy.239, f32[2,128]{1,0:T(2,128)S(1)} %get-tuple-element.210, ...), kind=kOutput, calls=%fused_computation.15.clone.1 | convolution fusion | flops 69009408 | bytes 572012 | tf_op jit(solution)/shard_map/while/body/eval_jaxpr/ljnq,ljqp->lnp/dot_general | solution.py:171
  229.6 0.8 gather_fusion
  231.7 4.6 %fusion.160 = f32[16,2,32,128]{3,2,1,0:T(8,128)} fusion(f32[16,2,32,128]{3,2,1,0:T(8,128)} %get-tuple-element.223, s32[]{:T(128)} %get-tuple-element.222, bf16[2,27,32,128]{3,2,1,0:T(8,128)(2,1)S(1)} %bitcast.270, f32[2,128]{1,0:T(2,128)S(1)} %get-tuple-element.206, f32[2,27,128]{2,1,0:T(8,128)S(1)} %copy.239, f32[2,128]{1,0:T(2,128)S(1)} %get-tuple-element.210, ...), kind=kOutput, calls=%fused_computation.15.clone.1 | convolution fusion | flops 69009408 | bytes 572012 | tf_op jit(solution)/shard_map/while/body/eval_jaxpr/ljnq,ljqp->lnp/dot_general | solution.py:171
  239.0 0.8 gather_fusion
  241.1 4.6 %fusion.160 = f32[16,2,32,128]{3,2,1,0:T(8,128)} fusion(f32[16,2,32,128]{3,2,1,0:T(8,128)} %get-tuple-element.223, s32[]{:T(128)} %get-tuple-element.222, bf16[2,27,32,128]{3,2,1,0:T(8,128)(2,1)S(1)} %bitcast.270, f32[2,128]{1,0:T(2,128)S(1)} %get-tuple-element.206, f32[2,27,128]{2,1,0:T(8,128)S(1)} %copy.239, f32[2,128]{1,0:T(2,128)S(1)} %get-tuple-element.210, ...), kind=kOutput, calls=%fused_computation.15.clone.1 | convolution fusion | flops 69009408 | bytes 572012 | tf_op jit(solution)/shard_map/while/body/eval_jaxpr/ljnq,ljqp->lnp/dot_general | solution.py:171
  248.5 0.8 gather_fusion
  250.5 4.6 %fusion.160 = f32[16,2,32,128]{3,2,1,0:T(8,128)} fusion(f32[16,2,32,128]{3,2,1,0:T(8,128)} %get-tuple-element.223, s32[]{:T(128)} %get-tuple-element.222, bf16[2,27,32,128]{3,2,1,0:T(8,128)(2,1)S(1)} %bitcast.270, f32[2,128]{1,0:T(2,128)S(1)} %get-tuple-element.206, f32[2,27,128]{2,1,0:T(8,128)S(1)} %copy.239, f32[2,128]{1,0:T(2,128)S(1)} %get-tuple-element.210, ...), kind=kOutput, calls=%fused_computation.15.clone.1 | convolution fusion | flops 69009408 | bytes 572012 | tf_op jit(solution)/shard_map/while/body/eval_jaxpr/ljnq,ljqp->lnp/dot_general | solution.py:171
  257.9 0.8 gather_fusion
  260.0 4.6 %fusion.160 = f32[16,2,32,128]{3,2,1,0:T(8,128)} fusion(f32[16,2,32,128]{3,2,1,0:T(8,128)} %get-tuple-element.223, s32[]{:T(128)} %get-tuple-element.222, bf16[2,27,32,128]{3,2,1,0:T(8,128)(2,1)S(1)} %bitcast.270, f32[2,128]{1,0:T(2,128)S(1)} %get-tuple-element.206, f32[2,27,128]{2,1,0:T(8,128)S(1)} %copy.239, f32[2,128]{1,0:T(2,128)S(1)} %get-tuple-element.210, ...), kind=kOutput, calls=%fused_computation.15.clone.1 | convolution fusion | flops 69009408 | bytes 572012 | tf_op jit(solution)/shard_map/while/body/eval_jaxpr/ljnq,ljqp->lnp/dot_general | solution.py:171
  264.6 1.0 copy_bitcast_fusion.5
  265.6 10.9 %fusion.17 = f32[32,64,32]{1,2,0:T(8,128)} fusion(bf16[32,6,64,32]{2,3,1,0:T(8,128)(2,1)S(1)} %bitcast.272, f32[32,64]{1,0:T(8,128)} %get-tuple-element.114, f32[32,6,64]{2,1,0:T(8,128)S(1)} %get-tuple-element.150, f32[32,64]{1,0:T(8,128)} %get-tuple-element.115, f32[32,6,64]{2,1,0:T(8,128)S(1)} %get-tuple-element.151, f32[32,64]{1,0:T(8,128)} %get-tuple-element.113, ...), kind=kOutput, calls=%fused_computation.34 | convolution fusion | flops 63700992 | bytes 1220992 | tf_op jit(solution)/shard_map/lfqp,lfqn->lpn/dot_general | solution.py:149
  276.5 1.9 fusion.21
  278.4 0.8 copy.218
  (343 shorter events, 85.5 us)
Async XLA Ops:
  0.0 23.9 %copy-start = (bf16[32,64,128]{2,1,0:T(8,128)(2,1)S(1)}, bf16[32,64,128]{2,1,0:T(8,128)(2,1)}, u32[]{:S(2)}) copy-start(bf16[32,64,128]{2,1,0:T(8,128)(2,1)} %param.19) | copy-start | bytes 1572868
  1.5 22.3 %copy-start.8 = (pred[32,128]{1,0:T(8,128)(4,1)}, pred[32,128]{1,0:T(8,128)(4,1)S(1)}, u32[]{:S(2)}) copy-start(pred[32,128]{1,0:T(8,128)(4,1)S(1)} %and_bitcast_fusion) | copy-start | bytes 12292
  23.9 1.2 copy-start.4
  24.3 16.8 %copy-start.2 = (bf16[32,64,64]{2,1,0:T(8,128)(2,1)S(1)}, bf16[32,64,64]{2,1,0:T(8,128)(2,1)}, u32[]{:S(2)}) copy-start(bf16[32,64,64]{2,1,0:T(8,128)(2,1)} %param.20) | copy-start | bytes 786436
  24.6 16.9 %copy-start.7 = (bf16[1,64,64]{2,1,0:T(8,128)(2,1)S(1)}, bf16[1,64,64]{2,1,0:T(8,128)(2,1)}, u32[]{:S(2)}) copy-start(bf16[1,64,64]{2,1,0:T(8,128)(2,1)} %param.21) | copy-start | bytes 24580
  25.1 82.2 %collective-permute-start.2 = (f32[32,2432]{1,0:T(8,128)S(1)}, f32[32,2432]{1,0:T(8,128)S(1)}, u32[]{:S(2)}, u32[]{:S(2)}) collective-permute-start(f32[32,2432]{1,0:T(8,128)S(1)} %constant_dynamic-update-slice_fusion), channel_id=1, source_target_pairs={{0,1},{1,2},{2,3},{3,4},{4,5},{5,6},{6,7},{7,8},{8,9},{9,10},{10,1... | collective-permute-start | bytes 933896 | tf_op jit(solution)/shard_map/ppermute | solution.py:20
  29.6 77.7 %collective-permute-start.3 = (f32[32,2432]{1,0:T(8,128)S(1)}, f32[32,2432]{1,0:T(8,128)S(1)}, u32[]{:S(2)}, u32[]{:S(2)}) collective-permute-start(f32[32,2432]{1,0:T(8,128)S(1)} %constant_dynamic-update-slice_fusion), channel_id=1, source_target_pairs={{1,0},{2,1},{3,2},{4,3},{5,4},{6,5},{7,6},{8,7},{9,8},{10,9},{11,1... | collective-permute-start | bytes 933896 | tf_op jit(solution)/shard_map/ppermute | solution.py:22
  31.7 74.5 %collective-permute-start = (bf16[32,4096]{1,0:T(8,128)(2,1)S(1)}, bf16[32,4096]{1,0:T(8,128)(2,1)}, u32[]{:S(2)}, u32[]{:S(2)}) collective-permute-start(bf16[32,4096]{1,0:T(8,128)(2,1)S(1)} %bitcast.284), channel_id=1, source_target_pairs={{0,1},{1,2},{2,3},{3,4},{4,5},{5,6},{6,7},{7,8},{8,9},{9,10},{10,1... | collective-permute-start | bytes 786440 | tf_op jit(solution)/shard_map/ppermute | solution.py:20
  35.3 71.8 %collective-permute-start.1 = (bf16[32,4096]{1,0:T(8,128)(2,1)S(1)}, bf16[32,4096]{1,0:T(8,128)(2,1)S(1)}, u32[]{:S(2)}, u32[]{:S(2)}) collective-permute-start(bf16[32,4096]{1,0:T(8,128)(2,1)S(1)} %bitcast.285), channel_id=1, source_target_pairs={{1,0},{2,1},{3,2},{4,3},{5,4},{6,5},{7,6},{8,7},{9,8},{10,9},{11,1... | collective-permute-start | bytes 786440 | tf_op jit(solution)/shard_map/ppermute | solution.py:22
  37.3 32.4 %copy-start.6 = (bf16[4,64,64]{2,1,0:T(8,128)(2,1)S(1)}, bf16[4,64,64]{2,1,0:T(8,128)(2,1)}, u32[]{:S(2)}) copy-start(bf16[4,64,64]{2,1,0:T(8,128)(2,1)} %param.22) | copy-start | bytes 98308
  38.0 29.2 %copy-start.10 = (s32[14]{0:T(128)S(1)}, s32[14]{0:T(128)}, u32[]{:S(2)}) copy-start(s32[14]{0:T(128)} %param.29) | copy-start | bytes 172
  74.1 18.7 %copy-start.12 = (s32[6]{0:T(128)S(1)}, s32[6]{0:T(128)}, u32[]{:S(2)}) copy-start(s32[6]{0:T(128)} %get-tuple-element.145) | copy-start | bytes 76
  92.8 12.7 %copy-start.11 = (s32[32]{0:T(128)S(1)}, s32[32]{0:T(128)}, u32[]{:S(2)}) copy-start(s32[32]{0:T(128)} %param.27) | copy-start | bytes 388
  113.6 151.9 %copy-start.1 = (bf16[192,64,32]{1,2,0:T(8,128)(2,1)S(1)}, bf16[192,64,32]{1,2,0:T(8,128)(2,1)}, u32[]{:S(2)}) copy-start(bf16[192,64,32]{1,2,0:T(8,128)(2,1)} %gather_fusion.4) | copy-start | bytes 2359300
  114.5 2.0 copy-start.5
  124.0 2.0 copy-start.5
  133.3 2.0 copy-start.5
  142.7 2.0 copy-start.5
  152.2 2.0 copy-start.5
  161.6 2.0 copy-start.5
  171.0 2.0 copy-start.5
  180.5 2.0 copy-start.5
  189.8 2.0 copy-start.5
  199.2 2.0 copy-start.5
  208.7 2.0 copy-start.5
  218.2 2.0 copy-start.5
  227.6 2.0 copy-start.5
  237.1 2.0 copy-start.5
  246.5 2.0 copy-start.5
  255.9 2.0 copy-start.5
  265.6 10.9 %copy-start.3 = (bf16[32,64,64]{2,1,0:T(8,128)(2,1)S(1)}, bf16[32,64,64]{2,1,0:T(8,128)(2,1)}, u32[]{:S(2)}) copy-start(bf16[32,64,64]{2,1,0:T(8,128)(2,1)} %param.20) | copy-start | bytes 786436
  265.6 10.9 %copy-start.9 = (bf16[64,32,1]{0,1,2:T(8,128)(2,1)S(1)}, bf16[64,32,1]{0,1,2:T(8,128)(2,1)}, u32[]{:S(2)}) copy-start(bf16[64,32,1]{0,1,2:T(8,128)(2,1)} %fusion.26) | copy-start | bytes 12292
where the time goes:
time: 282 us; the launch traced here: 279 us
  local copies, waits for them, and re-layouts  109 us (39%)
  matrix products  90.8 us (32%)
  blocking collectives  43.9 us (16%)
  other arithmetic  22.1 us (8%)
  starting transfers between devices  12 us (4%)
    dot_general x16, matrix products, near_block(): jnp.einsum('ljnq,ljqp->lnp', gathered, kernel, preferred_element_type=jnp...  73.2 us
    all_gather x1, blocking collectives, shards(): lax.all_gather(lifted.reshape(1, -1), ('br', 'sub'), axis=0, tiled=True)  22.4 us
    all_gather x1, blocking collectives, shards(): lax.all_gather(device_up.reshape(1, -1), ('br', 'sub'), axis=0, tiled=True)  18 us
    gather x2, local copies, waits for them, and re-layouts, shards(): jnp.take(branch_charges, order, axis=1)  16.6 us
    gather x16, local copies, waits for them, and re-layouts, near_block(): gathered = wide_charges[sources]  12.1 us
    sub x36, local copies, waits for them, and re-layouts, matern(): gap_first = sources[..., 0, :, None] - targets[..., 0, None, :]  11.9 us
    broadcast_in_dim x16, local copies, waits for them, and re-layouts, near_block(): targets[:, None]  11 us
    dot_general x1, matrix products, shards(): jnp.einsum('lfqp,lfqn->lpn', far_kernel, wide_coef[far_local], preferred_...  10.9 us
  transfers between devices with their start and end apart: 4, of which 0 were waited for; matrix products, arithmetic and copies ran while one was open for 11% of the time, Pallas kernels for 0%

commit v1 on v0

v1 whole, which is shorter than its diff:
```python
import functools
import math

import jax
import jax.numpy as jnp
from jax import lax
from jax.experimental import pallas as pl
from jax.experimental.pallas import tpu as pltpu
from jax.sharding import PartitionSpec as P

scale = 1.7320508075688772 / 0.25
f32 = jnp.float32
bf16 = jnp.bfloat16
HIGHEST = lax.Precision.HIGHEST
NT = (((1,), (1,)), ((), ()))
Q = 4
UNROLL = 4
FEAT = 16
CHUNK = 256
VMEM = pl.BlockSpec(memory_space=pltpu.VMEM)
SMEM = pl.BlockSpec(memory_space=pltpu.SMEM)
params = pltpu.CompilerParams(vmem_limit_bytes=50 << 20)


def profile_of(squared):
    squared = jnp.maximum(squared, 1e-12)
    scaled = squared * lax.rsqrt(squared)
    return (1.0 + scaled) * jnp.exp(-scaled)


def split(x):
    first = x.astype(bf16).astype(f32)
    rest = x - first
    second = rest.astype(bf16).astype(f32)
    return first, second, (rest - second).astype(bf16).astype(f32)


def permute_step(c, rows, order, base, start, rhs):
    per = CHUNK // order.shape[1]
    where_from = jnp.concatenate([order[pl.ds(c * per + i, 1), :] for i in range(per)], axis=1) - base
    low = where_from & (CHUNK - 1)
    high = where_from >> (CHUNK.bit_length() - 1)
    one_hot = jnp.where(
        lax.broadcasted_iota(jnp.int32, (CHUNK, CHUNK), 0) == low, 1.0, 0.0
    ).astype(bf16)
    picked = jnp.dot(rows[...], one_hot, preferred_element_type=f32)
    found = start
    for h in range(rows.shape[0] // rhs):
        found = jnp.where(high == h, picked[h * rhs : (h + 1) * rhs], found)
    return found


def prepare(
    near_src, near_count, charges, order, coords, part, feats, target, near_tab, far_tab, counts, rows, wide, tall
):
    leaves, points = order.shape
    rhs = charges.shape[0]
    near = near_src.shape[1]
    device = lax.axis_index(("br", "sub"))
    first = device * leaves
    base = lax.axis_index("sub") * (leaves * points)
    blocks = charges.shape[1] // CHUNK
    for h in range(blocks):
        rows[h * rhs : (h + 1) * rhs, :] = charges[:, h * CHUNK : (h + 1) * CHUNK]
    place = (coords[...] - 0.5) * scale
    r1, r2, r3 = split(place)
    n1, n2, n3 = split(
        place[0:1] * place[0:1] + place[1:2] * place[1:2] + place[2:3] * place[2:3]
    )
    one = jnp.ones_like(n1)
    wide[...] = jnp.zeros_like(wide)
    wide[0:3, :] = -2.0 * r1
    wide[3:6, :] = -2.0 * r2
    wide[6:9, :] = -2.0 * r3
    wide[9:10, :] = n1
    wide[10:11, :] = n2
    wide[11:12, :] = n3
    wide[12:13, :] = one
    feats[...] = wide[...].astype(bf16)
    tall[...] = jnp.zeros_like(tall)
    for i in range(3):
        tall[3 * i : 3 * i + 3, :] = r1
        tall[9 + i : 10 + i, :] = one
    tall[12:13, :] = n1
    tall[16:19, :] = r2
    tall[19:22, :] = r2
    tall[28:29, :] = n2
    tall[32:35, :] = r3
    tall[44:45, :] = n3
    lead = 4 * Q
    for i in range(lead):
        near_tab[i] = leaves
        far_tab[i] = 3 * leaves
    per = CHUNK // points

    def step(c, ends):
        near_end, far_end = ends
        at = pl.multiple_of(c * CHUNK, CHUNK)
        found = permute_step(c, rows, order, base, jnp.zeros((rhs, CHUNK), f32), rhs)
        part[:, pl.ds(at, CHUNK)] = found.astype(bf16)
        for i in range(per):
            leaf = c * per + i
            col = pl.multiple_of(leaf * points, points)
            target[pl.ds(col, points), :] = tall[:, pl.ds(col, points)].T.astype(bf16)
            code = leaf * 128
            live = near_count[leaf]
            for j in range(near):
                offset = near_src[leaf, j] - first
                valid = j < live
                local = (offset >= 0) & (offset < leaves)
                near_tab[near_end] = code + offset
                far_tab[far_end] = code + offset + leaves
                near_end = near_end + jnp.where(local & valid, 1, 0)
                far_end = far_end + jnp.where(valid & jnp.logical_not(local), 1, 0)
            near_tab[near_end] = code + leaves
            far_tab[far_end] = code + 3 * leaves
            near_end = near_end + (near_end & 1)
            far_end = far_end + (far_end & 1)
        return near_end, far_end

    near_end, far_end = lax.fori_loop(0, blocks, step, (jnp.int32(lead), jnp.int32(lead)))
    counts[0] = (near_end - lead) >> 1
    counts[1] = (far_end - lead) >> 1

    def fill(i, _):
        near_tab[near_end + i] = leaves
        far_tab[far_end + i] = 3 * leaves
        return 0

    lax.fori_loop(0, tail_length(), fill, 0)


def tail_length():
    return 2 * Q * (UNROLL + 4)


def table_length(leaves, near):
    need = 4 * Q + leaves * (near + near % 2) + tail_length()
    return -(-need // 128) * 128


def upward(part, charges, order, feats, basis, transfer, branch_transfer, upper_transfer, pack, up, rows):
    leaves, points = order.shape
    rhs = charges.shape[0]
    rank = basis.shape[1]
    base = (1 - lax.axis_index("sub")) * (leaves * points)
    blocks = charges.shape[1] // CHUNK
    for h in range(blocks):
        rows[h * rhs : (h + 1) * rhs, :] = charges[:, h * CHUNK : (h + 1) * CHUNK]
    pack[rhs : rhs + FEAT, :] = feats[...]

    def step(c, _):
        at = pl.multiple_of(c * CHUNK, CHUNK)
        found = permute_step(c, rows, order, base, part[:, pl.ds(at, CHUNK)].astype(f32), rhs)
        pack[0:rhs, pl.ds(at, CHUNK)] = found.astype(bf16)
        return 0

    lax.fori_loop(0, blocks, step, 0)
    lane = lax.broadcasted_iota(jnp.int32, (rhs, 2 * rank), 1)
    total = jnp.zeros((rhs, rank), f32)
    half = rhs // 2
    for i in range(leaves // 2):
        two = jnp.concatenate(
            [pack[0:rhs, (2 * i + k) * points : (2 * i + k + 1) * points] for k in range(2)], axis=0
        )
        weights = basis[2 * i : 2 * i + 2].reshape(2 * rank, points)
        both = lax.dot_general(two, weights, NT, preferred_element_type=f32)
        coef = jnp.where(lane < rank, both[:rhs], both[rhs:]).astype(bf16)
        at = i * 2 * rank
        pack[rhs + FEAT : rhs + FEAT + half, at : at + 2 * rank] = coef[:half]
        pack[rhs + FEAT : rhs + FEAT + half, leaves * rank + at : leaves * rank + at + 2 * rank] = coef[half:]
        total += jnp.dot(
            coef, transfer[2 * i : 2 * i + 2].reshape(2 * rank, rank), preferred_element_type=f32
        )
    lifted = jnp.dot(total, branch_transfer[0].astype(f32), precision=HIGHEST)
    parent = lax.axis_index("br") // 2
    second = jnp.dot(lifted, upper_transfer[parent].astype(f32), precision=HIGHEST)
    up[0:rhs, 0:rank] = total
    up[0:rhs, rank : 2 * rank] = lifted
    up[rhs : rhs + half, 0:rank] = second[:half]
    up[rhs : rhs + half, rank : 2 * rank] = second[half:]


def near_items(tab, pairs, target, sources, values, out, distances, kernels, points):
    total = (pairs + Q - 1) // Q
    for ref in distances + kernels:
        ref[...] = jnp.zeros_like(ref)

    def columns(leaf):
        return pl.ds(pl.multiple_of(leaf * points, points), points)

    def decode(item, q):
        one, two = tab[(item * Q + q) * 2], tab[(item * Q + q) * 2 + 1]
        return columns(one >> 7), columns(one & 127), columns(two & 127)

    def measure(item, distance):
        for q in range(Q):
            leaf, one, two = decode(item, q)
            pair = jnp.concatenate([sources[:, one], sources[:, two]], axis=1)
            distance[:, 2 * q * points : 2 * (q + 1) * points] = jnp.dot(
                target[leaf, :], jnp.concatenate([pair, pair, pair], axis=0), preferred_element_type=f32
            )

    def apply(item, kernel):
        sums = []
        for q in range(Q):
            leaf, one, two = decode(item, q)
            pair = jnp.concatenate([values[:, one], values[:, two]], axis=1)
            sums.append(
                (
                    leaf,
                    lax.dot_general(
                        pair,
                        kernel[:, 2 * q * points : 2 * (q + 1) * points],
                        NT,
                        preferred_element_type=f32,
                    ),
                )
            )
        for leaf, value in sums:
            out[:, leaf] += value

    def step(i, _):
        for u in range(UNROLL):
            item = i * UNROLL + u
            behind, last = (u - 1) % UNROLL, (u - 2) % UNROLL
            apply(item, kernels[last])
            kernels[behind][...] = profile_of(distances[behind][...]).astype(bf16)
            measure(item + 2, distances[u])
        return 0

    lax.fori_loop(0, (total + 2 + UNROLL - 1) // UNROLL, step, 0)


def near_local(tab, counts, pack, target, out, sources, values, *scratch):
    rhs, width = out.shape
    leaves = width // 128
    sources[:, :width] = pack[rhs : rhs + FEAT, :]
    sources[:, width:] = jnp.zeros_like(sources[:, width:])
    values[:, :width] = pack[0:rhs, :]
    values[:, width:] = jnp.zeros_like(values[:, width:])
    out[...] = jnp.zeros_like(out)
    near_items(
        tab, counts[0], target, sources, values, out, scratch[:UNROLL], scratch[UNROLL:], width // leaves
    )


def near_remote(
    tab, counts, far_src, far_count, before, pack, after, target, start, out, field,
    sources, values, low_sources, high_sources, low_values, high_values, *scratch
):
    rhs, width = out.shape
    leaves, far = far_src.shape
    points = width // leaves
    rank = field.shape[1] // leaves
    half = rhs // 2
    end = 3 * width
    for k, ref in enumerate((before, pack, after)):
        sources[:, k * width : (k + 1) * width] = ref[rhs : rhs + FEAT, :]
        values[:, k * width : (k + 1) * width] = ref[0:rhs, :]
    for ref in (sources, values, low_sources, high_sources, low_values, high_values):
        ref[:, end:] = jnp.zeros_like(ref[:, end:])
    out[...] = start[...]
    near_items(tab, counts[1], target, sources, values, out, scratch[:UNROLL], scratch[UNROLL:], points)
    early = lax.broadcasted_iota(jnp.int32, (FEAT, points), 1) < rank
    early_values = lax.broadcasted_iota(jnp.int32, (rhs, points), 1) < rank
    for k, ref in enumerate((before, pack, after)):
        for i in range(leaves // 2):
            at = i * points
            block = jnp.concatenate(
                [
                    ref[rhs + FEAT : rhs + FEAT + half, at : at + points],
                    ref[rhs + FEAT : rhs + FEAT + half, leaves * rank + at : leaves * rank + at + points],
                ],
                axis=0,
            ).astype(f32)
            turned = pltpu.roll(block, rank, 1)
            to = k * width + 2 * i * points
            low_values[:, to : to + points] = jnp.where(early_values, block, 0.0).astype(bf16)
            high_values[:, to : to + points] = jnp.where(early_values, 0.0, turned).astype(bf16)
            to += points
            low_values[:, to : to + points] = jnp.where(early_values, turned, 0.0).astype(bf16)
            high_values[:, to : to + points] = jnp.where(early_values, 0.0, block).astype(bf16)
        for i in range(leaves):
            to = k * width + i * points
            block = ref[rhs : rhs + FEAT, i * points : (i + 1) * points].astype(f32)
            turned = pltpu.roll(block, rank, 1)
            low_sources[:, to : to + points] = jnp.where(early, block, 0.0).astype(bf16)
            high_sources[:, to : to + points] = jnp.where(early, 0.0, turned).astype(bf16)
    base = (lax.axis_index(("br", "sub")) - 1) * leaves
    groups = (far + 1) // 2

    def columns(leaf):
        return pl.ds(pl.multiple_of(leaf * points, points), points)

    def far_leaf(leaf):
        live = far_count[leaf]
        places, coefs = [], []
        for g in range(groups):
            picked = []
            for j in (2 * g, 2 * g + 1):
                if j < far:
                    picked.append(jnp.where(j < live, far_src[leaf, j] - base, 3 * leaves))
                else:
                    picked.append(jnp.int32(3 * leaves))
            one, two = columns(picked[0]), columns(picked[1])
            places.append(low_sources[:, one] + high_sources[:, two])
            coefs.append(low_values[:, one] + high_values[:, two])
        places = jnp.concatenate(places, axis=1)
        rows = target[pl.ds(pl.multiple_of(leaf * points, points), rank), :]
        distance = jnp.dot(rows, jnp.concatenate([places] * 3, axis=0), preferred_element_type=f32)
        return profile_of(distance).astype(bf16), jnp.concatenate(coefs, axis=1)

    def far_step(i, _):
        for u in range(4):
            pair = i * 4 + u
            kernel_one, coef_one = far_leaf(2 * pair)
            kernel_two, coef_two = far_leaf(2 * pair + 1)
            both = lax.dot_general(
                jnp.concatenate([coef_one, coef_two], axis=0),
                jnp.concatenate([kernel_one, kernel_two], axis=0),
                NT,
                preferred_element_type=f32,
            )
            field[:, columns(pair)] = jnp.where(early_values, both[:rhs], both[rhs:])
        return 0

    lax.fori_loop(0, leaves // 8, far_step, 0)


def downward(
    top_src, top_count, every, skeleton, near, field, basis, transfer, branch_transfer, upper_transfer, out, places
):
    rhs = near.shape[0]
    leaves, rank, points = basis.shape
    subs = lax.axis_size("sub")
    branches = lax.axis_size("br")
    branch = lax.axis_index("br")
    depth = every.shape[0] // (branches * subs)
    half = rhs // 2
    fan = top_src.shape[1]

    def node_places(node):
        both = skeleton[:, pl.ds(pl.multiple_of((node >> 1) * (2 * rank), 2 * rank), 2 * rank)]
        return jnp.where((node & 1) == 1, both[:, rank:], both[:, :rank])

    def coefficients(level, node):
        devices = subs << level
        first = node * devices
        total = None
        for d in range(devices):
            at = pl.multiple_of((first + d) * depth, 8)
            if level < 2:
                block = every[pl.ds(at, rhs), :]
            else:
                block = every[pl.ds(at + rhs, half), :]
            total = block if total is None else total + block
        if level == 0:
            return total[:, :rank]
        if level == 1:
            return total[:, rank:]
        return jnp.concatenate([total[:, :rank], total[:, rank:]], axis=0)

    offset = 0
    fields = []
    for level in range(3):
        node = branch >> level
        row = offset + node
        places[0:3, 0:rank] = node_places(row)
        own = places[...].T
        kernels, coefs = [], []
        for j in range(fan):
            source = top_src[row, j]
            there = node_places(offset + source)
            squared = None
            for d in range(3):
                gap = (there[d : d + 1, :] - own[0:rank, d : d + 1]) * scale
                squared = gap * gap if squared is None else squared + gap * gap
            kernels.append(profile_of(squared))
            coefs.append(jnp.where(j < top_count[row], coefficients(level, source), 0.0))
        fields.append(
            lax.dot_general(
                jnp.concatenate(coefs, axis=1),
                jnp.concatenate(kernels, axis=1),
                NT,
                precision=HIGHEST,
                preferred_element_type=f32,
            )
        )
        offset += branches >> level
    down_one = fields[1] + lax.dot_general(
        fields[2], upper_transfer[branch >> 1].astype(f32), NT, precision=HIGHEST, preferred_element_type=f32
    )
    down_zero = fields[0] + lax.dot_general(
        down_one, branch_transfer[0].astype(f32), NT, precision=HIGHEST, preferred_element_type=f32
    )
    down_zero = down_zero.astype(bf16)
    lane = lax.broadcasted_iota(jnp.int32, (rhs, 2 * rank), 1)
    for i in range(leaves // 2):
        at = 2 * i * rank
        down = field[:, at : at + 2 * rank] + lax.dot_general(
            down_zero,
            transfer[2 * i : 2 * i + 2].reshape(2 * rank, rank),
            NT,
            preferred_element_type=f32,
        )
        both = jnp.concatenate(
            [jnp.where(lane < rank, down, 0.0), jnp.where(lane < rank, 0.0, down)], axis=0
        ).astype(bf16)
        value = jnp.dot(both, basis[2 * i : 2 * i + 2].reshape(2 * rank, points), preferred_element_type=f32)
        for k in range(2):
            col = (2 * i + k) * points
            out[:, col : col + points] = near[:, col : col + points] + value[k * rhs : (k + 1) * rhs]


def shards(
    charges,
    order,
    coords,
    leaf_basis,
    leaf_transfer,
    branch_transfer,
    upper_transfer,
    top_skeleton,
    near_src,
    near_count,
    far_src,
    far_count,
    top_src,
    top_count,
):
    rhs, width = charges.shape
    leaves, rank, points = leaf_basis.shape
    near = near_src.shape[1]
    subs = lax.axis_size("sub")
    devices = lax.axis_size(("br", "sub"))
    table = table_length(leaves, near)
    shape = jax.ShapeDtypeStruct
    cost = lambda us: pl.CostEstimate(
        flops=int(us * 1e6), bytes_accessed=int(us * 3e6), transcendentals=0
    )
    own_rows = order.reshape(leaves, points)
    partner = lax.ppermute(charges, "sub", [(i, (i + 1) % subs) for i in range(subs)])
    part, feats, target, near_tab, far_tab, counts = pl.pallas_call(
        prepare,
        out_shape=(
            shape((rhs, width), bf16),
            shape((FEAT, width), bf16),
            shape((width, 3 * FEAT), bf16),
            shape((table,), jnp.int32),
            shape((table,), jnp.int32),
            shape((2,), jnp.int32),
        ),
        in_specs=[SMEM, SMEM, VMEM, VMEM, VMEM],
        out_specs=(VMEM, VMEM, VMEM, SMEM, SMEM, SMEM),
        scratch_shapes=[
            pltpu.VMEM((rhs * width // CHUNK, CHUNK), bf16),
            pltpu.VMEM((FEAT, width), f32),
            pltpu.VMEM((3 * FEAT, width), f32),
        ],
        compiler_params=params,
        cost_estimate=cost(4),
        name="prepare",
    )(near_src, near_count, charges, own_rows, coords)
    pack, up = pl.pallas_call(
        upward,
        out_shape=(shape((rhs + FEAT + rhs // 2, width), bf16), shape((rhs + rhs // 2, 2 * rank), f32)),
        in_specs=[VMEM] * 8,
        out_specs=(VMEM, VMEM),
        scratch_shapes=[pltpu.VMEM((rhs * width // CHUNK, CHUNK), bf16)],
        compiler_params=params,
        cost_estimate=cost(4),
        name="upward",
    )(part, partner, own_rows, feats, leaf_basis, leaf_transfer, branch_transfer, upper_transfer)
    every = lax.all_gather(up, ("br", "sub"), axis=0, tiled=True)
    before = lax.ppermute(pack, ("br", "sub"), [(i, i + 1) for i in range(devices - 1)])
    after = lax.ppermute(pack, ("br", "sub"), [(i + 1, i) for i in range(devices - 1)])
    pipeline = [pltpu.VMEM((points, 2 * Q * points), f32)] * UNROLL + [
        pltpu.VMEM((points, 2 * Q * points), bf16)
    ] * UNROLL
    local = pl.pallas_call(
        near_local,
        out_shape=shape((rhs, width), f32),
        in_specs=[SMEM, SMEM, VMEM, VMEM],
        out_specs=VMEM,
        scratch_shapes=[
            pltpu.VMEM((FEAT, width + points), bf16),
            pltpu.VMEM((rhs, width + points), bf16),
        ]
        + pipeline,
        compiler_params=params,
        cost_estimate=cost(12),
        name="near_local",
    )(near_tab, counts, pack, target)
    both, field = pl.pallas_call(
        near_remote,
        out_shape=(shape((rhs, width), f32), shape((rhs, leaves * rank), f32)),
        in_specs=[SMEM] * 4 + [VMEM] * 5,
        out_specs=(VMEM, VMEM),
        scratch_shapes=[
            pltpu.VMEM((FEAT, 3 * width + points), bf16),
            pltpu.VMEM((rhs, 3 * width + points), bf16),
            pltpu.VMEM((FEAT, 3 * width + points), bf16),
            pltpu.VMEM((FEAT, 3 * width + points), bf16),
            pltpu.VMEM((rhs, 3 * width + points), bf16),
            pltpu.VMEM((rhs, 3 * width + points), bf16),
        ]
        + pipeline,
        compiler_params=params,
        cost_estimate=cost(14),
        name="near_remote",
    )(far_tab, counts, far_src, far_count, before, pack, after, target, local)
    return pl.pallas_call(
        downward,
        out_shape=shape((rhs, width), f32),
        in_specs=[SMEM, SMEM] + [VMEM] * 8,
        out_specs=VMEM,
        scratch_shapes=[pltpu.VMEM((8, 128), f32)],
        compiler_params=params,
        cost_estimate=cost(4),
        name="downward",
    )(
        top_src,
        top_count,
        every,
        top_skeleton,
        both,
        field,
        leaf_basis,
        leaf_transfer,
        branch_transfer,
        upper_transfer,
    )


def solution(mesh):
    return jax.shard_map(
        shards,
        mesh=mesh,
        in_specs=(
            P(None, ("grp", "br", "sub")),
            P(("grp", "br", "sub")),
            P(None, ("grp", "br", "sub")),
            P(("grp", "br", "sub"), None, None),
            P(("grp", "br", "sub"), None, None),
            P(("grp", "br"), None, None),
            P("grp", None, None),
            P(None, "grp"),
            P(("grp", "br", "sub"), None),
            P(("grp", "br", "sub")),
            P(("grp", "br", "sub"), None),
            P(("grp", "br", "sub")),
            P("grp", None),
            P("grp"),
        ),
        out_specs=P(None, ("grp", "br", "sub")),
        check_vma=False,
    )
```

time: 282 us -> 84.5 us (0.30)
  local copies, waits for them, and re-layouts: 109 us -> 7.37 us
  matrix products: 90.8 us -> 0 us
  Pallas kernels: 0 us -> 47.5 us
  other arithmetic: 22.1 us -> 0 us
  blocking collectives: 43.9 us -> 22.3 us
  starting transfers between devices: 12 us -> 6.62 us
    dot_general x27 -> x0, matrix products: 90.8 us -> none  [the longest x16 73.2 us: near_block(): jnp.einsum('ljnq,ljqp->lnp', gathered, kernel, preferred_element_type=jnp...]
    pallas_call x0 -> x5, Pallas kernels: none -> 47.5 us  [the longest x1 15.5 us: shards(): pl.pallas_call(near_remote, out_shape=(shape((rhs, width), f32), shape((r...]
    gather x42 -> x0, local copies, waits for them, and re-layouts: 45.4 us -> none  [the longest x2 16.6 us: shards(): jnp.take(branch_charges, order, axis=1)]
    sub x85 -> x0, local copies, waits for them, and re-layouts: 23.1 us -> none  [the longest x36 11.9 us: matern(): gap_first = sources[..., 0, :, None] - targets[..., 0, None, :]]
    all_gather x3 -> x1, blocking collectives: 43.9 us -> 22.3 us  [shards(): every = lax.all_gather(up, ('br', 'sub'), axis=0, tiled=True)]
    select_n x20 -> x0, other arithmetic: 11.9 us -> none  [the longest x16 10.7 us: near_block(): gathered = wide_charges[sources]]
    broadcast_in_dim x18 -> x0, local copies, waits for them, and re-layouts: 11.1 us -> none  [the longest x16 11 us: near_block(): targets[:, None]]
    mul x16 -> x0, local copies, waits for them, and re-layouts: 10.3 us -> none  [near_block(): matern(wide_places[sources], targets[:, None]).astype(jnp.bfloat16)]
  transfers between devices with their start and end apart: 4 -> 3, of which waited for: 0 -> 0; matrix products, arithmetic and copies ran while one was open for 11% -> 0% of each run, Pallas kernels for 0% -> 26%
where the time goes in v1:
time: 84.5 us; the launch traced here: 83.9 us
  Pallas kernels  47.5 us (56%)
  blocking collectives  22.3 us (26%)
  local copies, waits for them, and re-layouts  7.37 us (9%)
  starting transfers between devices  6.62 us (8%)
    all_gather x1, blocking collectives, shards(): every = lax.all_gather(up, ('br', 'sub'), axis=0, tiled=True)  22.3 us
    pallas_call x1, Pallas kernels, shards(): pl.pallas_call(near_remote, out_shape=(shape((rhs, width), f32), shape((r...  15.5 us
    pallas_call x1, Pallas kernels, shards(): pl.pallas_call(near_local, out_shape=shape((rhs, width), f32), in_specs=[...  12.5 us
    pallas_call x1, Pallas kernels, shards(): pl.pallas_call(prepare, out_shape=(shape((rhs, width), bf16), shape((FEAT...  8.94 us
    unnamed x34, local copies, waits for them, and re-layouts  7.37 us
    pallas_call x1, Pallas kernels, shards(): pl.pallas_call(downward, out_shape=shape((rhs, width), f32), in_specs=[SM...  5.31 us
    pallas_call x1, Pallas kernels, shards(): pl.pallas_call(upward, out_shape=(shape((rhs + FEAT + rhs // 2, width), b...  5.27 us
    ppermute x1, starting transfers between devices, shards(): lax.ppermute(pack, ('br', 'sub'), [(i, i + 1) for i in range(devices - 1)])  4.64 us
  transfers between devices with their start and end apart: 3, of which 0 were waited for; matrix products, arithmetic and copies ran while one was open for 0% of the time, Pallas kernels for 26%

profile of v1, /device:TPU:1, one launch (start us, length us, event | category | flops | bytes accessed | tf_op | source)
XLA Modules:
  0.0 83.9 jit_solution(5323325200328193234)
XLA Ops:
  0.0 0.0 copy-start.11
  0.0 0.1 collective-permute-start
  0.1 0.6 copy-done.11
  0.7 0.0 copy-start.5
  0.7 0.9 %copy-done.5 = bf16[32,4096]{1,0:T(8,128)(2,1)S(1)} copy-done((bf16[32,4096]{1,0:T(8,128)(2,1)S(1)}, bf16[32,4096]{1,0:T(8,128)(2,1)}, u32[]{:S(2)}) %copy-start.5) | copy-done | bytes 262168
  1.6 0.0 copy-start.7
  1.6 0.7 copy-done.7
  2.3 0.0 copy-start.8
  2.3 0.8 copy-done.8
  3.2 0.0 copy-start.9
  3.2 0.7 copy-done.9
  3.9 0.0 copy-start.4
  3.9 0.0 copy-start.6
  3.9 8.9 %prepare.1 = (bf16[32,4096]{1,0:T(8,128)(2,1)S(1)}, bf16[16,4096]{1,0:T(8,128)(2,1)S(1)}, bf16[4096,48]{1,0:T(8,128)(2,1)S(1)}, s32[1024]{0:T(1024)S(1)}, s32[1024]{0:T(1024)S(1)}, /*index=5*/s32[2]{0:T(128)S(1)}) custom-call(s32[32,27]{1,0:T(8,128)S(1)} %copy-done.9, s32[32]{0:T(128)S(1)} %copy-done.11, bf16[32,4096]{1,0:T(8,128)(2,1)S(1)} %copy-done.5, ...), custom_call_target="tpu_custom_call" | custom-call | flops 4000000 | bytes 12000000 | tf_op jit(solution)/shard_map/prepare/pallas_call | solution.py:444
  12.8 0.0 collective-permute-done.charges
  12.8 0.0 copy-done.4
  12.9 0.0 copy-done.6
  12.9 0.0 copy-start
  12.9 1.0 %copy-done = bf16[32,64,128]{2,1,0:T(8,128)(2,1)S(1)} copy-done((bf16[32,64,128]{2,1,0:T(8,128)(2,1)S(1)}, bf16[32,64,128]{2,1,0:T(8,128)(2,1)}, u32[]{:S(2)}) %copy-start) | copy-done | bytes 524312
  13.9 0.0 copy-start.2
  13.9 1.0 %copy-done.2 = bf16[32,64,64]{2,1,0:T(8,128)(2,1)S(1)} copy-done((bf16[32,64,64]{2,1,0:T(8,128)(2,1)S(1)}, bf16[32,64,64]{2,1,0:T(8,128)(2,1)}, u32[]{:S(2)}) %copy-start.2) | copy-done | bytes 262168
  14.9 0.0 copy-start.14
  15.0 5.3 %upward.1 = (bf16[64,4096]{1,0:T(8,128)(2,1)S(1)}, f32[48,128]{1,0:T(8,128)S(1)}) custom-call(bf16[32,4096]{1,0:T(8,128)(2,1)S(1)} %get-tuple-element.15.part, bf16[32,4096]{1,0:T(8,128)(2,1)S(1)} %collective-permute-done.charges, s32[32,128]{1,0:T(8,128)S(1)} %bitcast.2, bf16[16,4096]{1,0:T(8,128)(2,1)S(1)} %get-tuple-element.16.feats, ...), custom_call_target="tpu_custom_call" | custom-call | flops 4000000 | bytes 12000000 | tf_op jit(solution)/shard_map/upward/pallas_call | solution.py:465
  20.2 0.0 copy-start.15
  20.2 4.6 %collective-permute-start.1 = (bf16[64,4096]{1,0:T(8,128)(2,1)S(1)}, bf16[64,4096]{1,0:T(8,128)(2,1)S(1)}, u32[]{:S(2)}, u32[]{:S(2)}) collective-permute-start(bf16[64,4096]{1,0:T(8,128)(2,1)S(1)} %get-tuple-element.20.pack), channel_id=1, source_target_pairs={{0,1},{1,2},{2,3},{3,4},{4,5},{5,6},{6,7},{7,8},{8,9},{9,10},{10,1... | collective-permute-start | bytes 1572872 | tf_op jit(solution)/shard_map/ppermute | solution.py:476
  24.9 1.9 %collective-permute-start.2 = (bf16[64,4096]{1,0:T(8,128)(2,1)S(1)}, bf16[64,4096]{1,0:T(8,128)(2,1)S(1)}, u32[]{:S(2)}, u32[]{:S(2)}) collective-permute-start(bf16[64,4096]{1,0:T(8,128)(2,1)S(1)} %get-tuple-element.20.pack), channel_id=1, source_target_pairs={{1,0},{2,1},{3,2},{4,3},{5,4},{6,5},{7,6},{8,7},{9,8},{10,9},{11,1... | collective-permute-start | bytes 1572872 | tf_op jit(solution)/shard_map/ppermute | solution.py:477
  26.8 0.0 copy-done.14
  26.8 0.1 copy.15.far_src
  26.9 0.0 copy-done.15
  26.9 0.1 copy.16.top_src
  27.0 12.5 %near_local.1.start = f32[32,4096]{1,0:T(8,128)S(1)} custom-call(s32[1024]{0:T(1024)S(1)} %get-tuple-element.22.tab, s32[2]{0:T(128)S(1)} %get-tuple-element.19.counts, bf16[64,4096]{1,0:T(8,128)(2,1)S(1)} %get-tuple-element.20.pack, bf16[4096,48]{1,0:T(8,128)(2,1)S(1)} %get-tuple-element.21.target), custom_call_target="tpu_custom_call" | custom-call | flops 12000000 | bytes 36000000 | tf_op jit(solution)/shard_map/near_local/pallas_call | solution.py:481
  39.5 22.3 %all_gather.3.every = f32[768,128]{1,0:T(8,128)S(1)} all-gather(f32[48,128]{1,0:T(8,128)S(1)} %get-tuple-element.17), channel_id=1, replica_groups=mesh['grp'=2,'br'=8,'sub'=2] {'br','sub'}, dimensions={0}, use_global_device_ids=true | all-gather | bytes 417792 | tf_op jit(solution)/shard_map/all_gather | solution.py:475
  61.8 0.0 copy-start.12
  61.8 0.0 collective-permute-done.1.before
  61.8 0.0 collective-permute-done.2.after
  61.8 0.6 copy-done.12
  62.4 0.0 copy-start.1
  62.4 0.0 copy-start.3
  62.4 0.0 copy-start.10
  62.4 15.5 %near_remote.1 = (f32[32,4096]{1,0:T(8,128)S(1)}, f32[32,2048]{1,0:T(8,128)S(1)}) custom-call(s32[1024]{0:T(1024)S(1)} %get-tuple-element.18.tab, s32[2]{0:T(128)S(1)} %get-tuple-element.19.counts, s32[32,6]{1,0:T(8,128)S(1)} %copy.15.far_src, s32[32]{0:T(128)S(1)} %copy-done.12, bf16[64,4096]{1,0:T(8,128)(2,1)S(1)} %collective-permute-done.1.before, ...), custom_call_target="tpu_custom_call" | custom-call | flops 14000000 | bytes 42000000 | tf_op jit(solution)/shard_map/near_remote/pallas_call | solution.py:495
  78.0 0.0 copy-start.13
  78.0 0.0 copy-done.1
  78.0 0.0 copy-done.3
  78.0 0.0 copy-done.10
  78.0 0.6 copy-done.13
  78.6 5.3 %downward.1 = f32[32,4096]{1,0:T(8,128)} custom-call(s32[14,6]{1,0:T(8,128)S(1)} %copy.16.top_src, s32[14]{0:T(128)S(1)} %copy-done.13, f32[768,128]{1,0:T(8,128)S(1)} %all_gather.3.every, f32[3,896]{1,0:T(4,128)S(1)} %copy-done.10, f32[32,4096]{1,0:T(8,128)S(1)} %get-tuple-element.23.near, f32[32,2048]{1,0:T(8,128)S(1)} %get-tuple-element.24.field, ...), custom_call_target="tpu_custom_call" | custom-call | flops 4000000 | bytes 12000000 | tf_op jit(solution)/shard_map/downward/pallas_call | solution.py:513
Async XLA Ops:
  0.0 0.7 copy-start.11
  0.0 12.8 %collective-permute-start = (bf16[32,4096]{1,0:T(8,128)(2,1)}, bf16[32,4096]{1,0:T(8,128)(2,1)S(1)}, u32[]{:S(2)}, u32[]{:S(2)}) collective-permute-start(bf16[32,4096]{1,0:T(8,128)(2,1)} %charges.1), channel_id=1, source_target_pairs={{0,1},{1,0},{2,3},{3,2},{4,5},{5,4},{6,7},{7,6},{8,9},{9,8},{10,11... | collective-permute-start | bytes 786440 | tf_op jit(solution)/shard_map/ppermute | solution.py:443
  0.7 0.9 %copy-start.5 = (bf16[32,4096]{1,0:T(8,128)(2,1)S(1)}, bf16[32,4096]{1,0:T(8,128)(2,1)}, u32[]{:S(2)}) copy-start(bf16[32,4096]{1,0:T(8,128)(2,1)} %charges.1) | copy-start | bytes 786436
  1.6 0.7 copy-start.7
  2.3 0.8 copy-start.8
  3.2 0.7 copy-start.9
  3.9 9.0 %copy-start.4 = (bf16[4,64,64]{2,1,0:T(8,128)(2,1)S(1)}, bf16[4,64,64]{2,1,0:T(8,128)(2,1)}, u32[]{:S(2)}) copy-start(bf16[4,64,64]{2,1,0:T(8,128)(2,1)} %upper_transfer.3) | copy-start | bytes 98308
  3.9 9.0 %copy-start.6 = (bf16[1,64,64]{2,1,0:T(8,128)(2,1)S(1)}, bf16[1,64,64]{2,1,0:T(8,128)(2,1)}, u32[]{:S(2)}) copy-start(bf16[1,64,64]{2,1,0:T(8,128)(2,1)} %branch_transfer.3) | copy-start | bytes 24580
  12.9 1.0 %copy-start = (bf16[32,64,128]{2,1,0:T(8,128)(2,1)S(1)}, bf16[32,64,128]{2,1,0:T(8,128)(2,1)}, u32[]{:S(2)}) copy-start(bf16[32,64,128]{2,1,0:T(8,128)(2,1)} %basis.3) | copy-start | bytes 1572868
  13.9 1.0 %copy-start.2 = (bf16[32,64,64]{2,1,0:T(8,128)(2,1)S(1)}, bf16[32,64,64]{2,1,0:T(8,128)(2,1)}, u32[]{:S(2)}) copy-start(bf16[32,64,64]{2,1,0:T(8,128)(2,1)} %transfer.3) | copy-start | bytes 786436
  14.9 11.9 %copy-start.14 = (s32[32,6]{0,1:T(8,128)S(1)}, s32[32,6]{0,1:T(8,128)}, u32[]{:S(2)}) copy-start(s32[32,6]{0,1:T(8,128)} %param.24) | copy-start | bytes 2308
  20.2 6.7 %copy-start.15 = (s32[14,6]{0,1:T(8,128)S(1)}, s32[14,6]{0,1:T(8,128)}, u32[]{:S(2)}) copy-start(s32[14,6]{0,1:T(8,128)} %param.26) | copy-start | bytes 1012
  20.2 41.5 %collective-permute-start.1 = (bf16[64,4096]{1,0:T(8,128)(2,1)S(1)}, bf16[64,4096]{1,0:T(8,128)(2,1)S(1)}, u32[]{:S(2)}, u32[]{:S(2)}) collective-permute-start(bf16[64,4096]{1,0:T(8,128)(2,1)S(1)} %get-tuple-element.20.pack), channel_id=1, source_target_pairs={{0,1},{1,2},{2,3},{3,4},{4,5},{5,6},{6,7},{7,8},{8,9},{9,10},{10,1... | collective-permute-start | bytes 1572872 | tf_op jit(solution)/shard_map/ppermute | solution.py:476
  24.9 36.9 %collective-permute-start.2 = (bf16[64,4096]{1,0:T(8,128)(2,1)S(1)}, bf16[64,4096]{1,0:T(8,128)(2,1)S(1)}, u32[]{:S(2)}, u32[]{:S(2)}) collective-permute-start(bf16[64,4096]{1,0:T(8,128)(2,1)S(1)} %get-tuple-element.20.pack), channel_id=1, source_target_pairs={{1,0},{2,1},{3,2},{4,3},{5,4},{6,5},{7,6},{8,7},{9,8},{10,9},{11,1... | collective-permute-start | bytes 1572872 | tf_op jit(solution)/shard_map/ppermute | solution.py:477
  61.8 0.7 copy-start.12
  62.4 15.6 %copy-start.1 = (bf16[32,64,128]{2,1,0:T(8,128)(2,1)S(1)}, bf16[32,64,128]{2,1,0:T(8,128)(2,1)}, u32[]{:S(2)}) copy-start(bf16[32,64,128]{2,1,0:T(8,128)(2,1)} %basis.3) | copy-start | bytes 1572868
  62.4 15.6 %copy-start.3 = (bf16[32,64,64]{2,1,0:T(8,128)(2,1)S(1)}, bf16[32,64,64]{2,1,0:T(8,128)(2,1)}, u32[]{:S(2)}) copy-start(bf16[32,64,64]{2,1,0:T(8,128)(2,1)} %transfer.3) | copy-start | bytes 786436
  62.4 15.6 %copy-start.10 = (f32[3,896]{1,0:T(4,128)S(1)}, f32[3,896]{1,0:T(4,128)}, u32[]{:S(2)}) copy-start(f32[3,896]{1,0:T(4,128)} %skeleton.1) | copy-start | bytes 32260
  78.0 0.7 copy-start.13
